TPU v7x, 256 devices: a whole 4x4x8 slice. The times are simulated.
256 devices in a mesh: expert: 32 (over z, y), dp: 8 (over x, core).
Axes of the slice: x: 4, y: 4, z: 8, core: 2. Of those that a mesh axis runs over, the one named last changes fastest.
Arguments:
- partial_grads: bfloat16 [8, 256, 2, 16, 7168], P('dp', 'expert'), may hold values from -6 to 6
- replica_grads: bfloat16 [8, 64, 16, 7168], P('dp', 'expert'), may hold values from -6 to 6
- replica_item: int32 [64], P('expert'), may hold values from 0 to 511
- weight: float32 [256, 2, 16, 7168], P('expert', None, None, 'dp'), may hold values from -0.125 to 0.125
- first_moment: float32 [256, 2, 16, 7168], P('expert', None, None, 'dp'), may hold values from -3 to 3
- second_moment: float32 [256, 2, 16, 7168], P('expert', None, None, 'dp'), may hold values from 0.05 to 5
- new_position: int32 [256, 2], P('expert'), may hold values from 0 to 511, as said below
Outputs:
- new_weight: float32 [256, 2, 16, 7168], P('expert', None, None, 'dp')
- new_first: float32 [256, 2, 16, 7168], P('expert', None, None, 'dp')
- new_second: float32 [256, 2, 16, 7168], P('expert', None, None, 'dp')
Inputs may be any that keep to these rules, and one draw needn't show every extreme that they name: new_position is a permutation of the 512 items; the items of one index of expert that go to any one index of expert (itself included) number at most 1, and exactly 1 for some pairs.
All inputs are finite; a program needn't handle non-finite values.
Results may differ from a plain program's by a relative error of at most 0.0003.
Values sent between devices are 32-bit elements; how exact they have to be, the bound alone decides.
A program may use at most 128 MiB of HBM per device.

v0:
```python
import jax
import jax.numpy as jnp
from jax import lax
from jax.sharding import PartitionSpec as P

STEP = 10


beta_one = 0.9
beta_two = 0.95
learn_rate = 0.003
decay_rate = 0.1
epsilon = 1e-08


def adam_update(weight, first_mom, second_mom, gradient):
    first_new = beta_one * first_mom + (1.0 - beta_one) * gradient
    second_new = beta_two * second_mom + (1.0 - beta_two) * gradient * gradient
    first_hat = first_new / (1.0 - beta_one**STEP)
    second_hat = second_new / (1.0 - beta_two**STEP)
    weight_new = weight - learn_rate * (
        first_hat / (jnp.sqrt(second_hat) + epsilon) + decay_rate * weight
    )
    return (weight_new, first_new, second_new)


def pack_slots(new_position, device_count):
    item_count = new_position.shape[0] * new_position.shape[1]
    target_pos = new_position.reshape(item_count)
    target_dev = target_pos // item_count
    capacity = max(1, item_count // device_count)
    indices = jnp.arange(item_count)
    earlier = (target_dev[:, None] == target_dev[None, :]) & (indices[None, :] < indices[:, None])
    order_rank = jnp.sum(earlier.astype(jnp.int32), axis=1)
    slot_index = target_dev * capacity + order_rank
    labels = jnp.full((device_count * capacity,), -1.0, jnp.float32)
    labels = labels.at[slot_index].set((target_pos % item_count).astype(jnp.float32))
    return (slot_index, labels, capacity)


def fill_slots(values, slot_index, slot_count):
    outgoing = jnp.zeros((slot_count,) + values.shape[1:], jnp.float32)
    return outgoing.at[slot_index].set(values)


def unpack_slots(received, labels, item_count):
    valid = labels >= 0.0
    target_row = jnp.where(valid, labels, float(item_count)).astype(jnp.int32)
    empty = jnp.zeros((item_count,) + received.shape[1:], received.dtype)
    return empty.at[target_row].set(received, mode="drop")


def per_device(
    partial_grads, replica_grads, replica_item, weight, first_moment, second_moment, new_position
):
    device_index = lax.axis_index("expert")
    device_count = lax.axis_size("expert")
    expert_count, layer_count, row_count, columns = weight.shape
    item_count = expert_count * layer_count
    summed, replica_sum = (
        lax.psum_scatter(
            partial_grads[0].astype(jnp.float32), "dp", scatter_dimension=3, tiled=True
        ),
        lax.psum_scatter(
            replica_grads[0].astype(jnp.float32), "dp", scatter_dimension=2, tiled=True
        ),
    )
    first_item = device_index * item_count
    flattened = summed.reshape(item_count, row_count, columns)
    values = lax.all_gather(replica_sum, "expert", axis=0, tiled=True)
    item_ids = lax.all_gather(replica_item.astype(jnp.float32), "expert", axis=0, tiled=True)
    local_ids = item_ids.astype(jnp.int32) - first_item
    inside = (local_ids >= 0) & (local_ids < item_count)
    gradient = flattened.at[jnp.where(inside, local_ids, item_count)].add(values, mode="drop")
    slot_index, labels, capacity = pack_slots(new_position, device_count)
    slot_count = device_count * capacity
    old_weight = weight.reshape(item_count, row_count, columns)
    old_first = first_moment.reshape(item_count, row_count, columns)
    old_second = second_moment.reshape(item_count, row_count, columns)
    upd_weight, upd_first, upd_second = adam_update(old_weight, old_first, old_second, gradient)
    states = jnp.stack([upd_weight, upd_first, upd_second], axis=1)
    outgoing = fill_slots(states, slot_index, slot_count)
    received, got_labels = (
        lax.all_to_all(outgoing, "expert", split_axis=0, concat_axis=0, tiled=True),
        lax.all_to_all(labels, "expert", split_axis=0, concat_axis=0, tiled=True),
    )
    placed = unpack_slots(received, got_labels, item_count)
    out_weight, out_first, out_second = (placed[:, 0], placed[:, 1], placed[:, 2])
    shape_out = (expert_count, layer_count, row_count, columns)
    return (
        out_weight.reshape(shape_out),
        out_first.reshape(shape_out),
        out_second.reshape(shape_out),
    )


def solution(mesh):
    in_specs = (
        P("dp", "expert", None, None, None),
        P("dp", "expert", None, None),
        P("expert"),
        P("expert", None, None, "dp"),
        P("expert", None, None, "dp"),
        P("expert", None, None, "dp"),
        P("expert", None),
    )
    out_specs = (
        P("expert", None, None, "dp"),
        P("expert", None, None, "dp"),
        P("expert", None, None, "dp"),
    )
    return jax.shard_map(
        per_device, mesh=mesh, in_specs=in_specs, out_specs=out_specs, check_vma=False
    )
```

profile of v0, /device:TPU:6, one launch (start us, length us, event | category | flops | bytes accessed | tf_op | source)
XLA Modules:
  0.0 349.8 jit_solution(12197076964610718880)
XLA Ops:
  7.2 0.0 reduce-scatter.5.cloned.1.call-start
  7.2 2.0 bitcast_convert_fusion.1
  9.2 0.0 all-gather.2.cloned.1.call-start
  9.3 35.8 %reduce-scatter.5.cloned.1.call-done = f32[2,16,896]{2,1,0:T(8,128)} async-done(((f32[2,16,7168]{2,1,0:T(8,128)}), f32[2,16,896]{2,1,0:T(8,128)}) %reduce-scatter.5.cloned.1.call-update) | async-done | bytes 114704 | tf_op jit(solution)/shard_map/reduce_scatter | solution.py:64
  45.1 0.0 reduce-scatter.3.cloned.1.call-start
  45.1 5.9 %bitcast_convert_fusion = f32[8,2,16,7168]{3,2,1,0:T(8,128)} fusion(bf16[1,8,2,16,7168]{4,3,2,1,0:T(8,128)(2,1)} %param.7), kind=kLoop, calls=%fused_computation.4 | loop fusion | flops 1835008 | bytes 11010048 | tf_op jit(solution)/shard_map/convert_element_type | solution.py:62
  51.0 0.0 reduce-scatter.3.cloned.1.call-update
  51.0 0.6 copy-done.2
  51.7 0.1 copy.28
  51.8 0.1 reshape.184
  51.9 0.1 reshape.183
  52.0 0.2 convert_reduce_fusion
  52.1 0.6 scatter_custom_fusion
  52.8 0.7 copy.30
  53.5 9.9 %all-to-all-start = ((f32[32,1,1]{2,1,0:T(1,128)}), f32[32,1,1]{2,1,0:T(1,128)S(1)}, u32[]{:S(2)}, u32[]{:S(2)}) async-start(f32[32,1,1]{2,1,0:T(1,128)} %copy.30), calls=%async_computation | async-start | bytes 32768 | tf_op jit(solution)/shard_map/all_to_all | solution.py:85
  63.4 0.6 dynamic-slice
  64.6 0.1 convert_dynamic-update-slice_fusion
  64.7 75.0 %all-reduce = f32[64]{0:T(128)S(1)} all-reduce(f32[64]{0:T(128)S(1)} %convert_dynamic-update-slice_fusion), channel_id=1, replica_groups=mesh['expert'=32,'dp'=8] {'expert'}, use_global_device_ids=true, to_apply=%add | all-reduce | flops 64 | bytes 512
  139.8 1.4 broadcast_multiply_fusion
  141.1 0.0 all-gather.2.cloned.1.call-done
  141.2 37.5 %reduce-scatter.3.cloned.1.call-done = f32[8,2,16,896]{3,2,1,0:T(8,128)} async-done(((f32[8,2,16,7168]{3,2,1,0:T(8,128)}), f32[8,2,16,896]{3,2,1,0:T(8,128)}) %reduce-scatter.3.cloned.1.call-update) | async-done | bytes 917520 | tf_op jit(solution)/shard_map/reduce_scatter | solution.py:61
  178.7 12.3 %scatter_fusion = f32[16,16,896]{2,1,0:T(8,128)} fusion(f32[16,16,896]{2,1,0:T(8,128)} %bitcast.44, s32[64]{0:T(128)S(1)} %compare_select_fusion, f32[64,16,896]{2,1,0:T(8,128)} %all-gather.2.cloned.1.call-done), kind=kCustom, calls=%fused_computation.1 | custom fusion | flops 917504 | bytes 11010304 | tf_op jit(solution)/shard_map/scatter-add | solution.py:74
  191.0 1.9 bitcast_subtract_fusion
  192.9 0.2 pad_maximum_fusion
  193.1 2.8 broadcast_in_dim.28
  195.9 4.2 %scatter_fusion.1 = f32[32,3,16,896]{3,2,1,0:T(8,128)} fusion(f32[32,3,16,896]{3,2,1,0:T(8,128)} %broadcast_in_dim.28, s32[16]{0:T(128)S(1)} %fusion.5, f32[16,3,16,896]{3,2,1,0:T(8,128)S(1)} %pad_maximum_fusion), kind=kCustom, calls=%fused_computation.2 | custom fusion | bytes 8257600 | tf_op jit(solution)/shard_map/scatter | solution.py:43
  200.1 9.8 %all-to-all-start.1 = ((f32[32,3,16,896]{3,2,1,0:T(8,128)}), f32[32,3,16,896]{3,2,1,0:T(8,128)}, u32[]{:S(2)}, u32[]{:S(2)}) async-start(f32[32,3,16,896]{3,2,1,0:T(8,128)} %scatter_fusion.1), calls=%async_computation.3 | async-start | bytes 11010048 | tf_op jit(solution)/shard_map/all_to_all | solution.py:84
  210.0 0.3 reduce
  210.3 126.0 %all-to-all-done.1 = f32[32,3,16,896]{3,2,1,0:T(8,128)} async-done(((f32[32,3,16,896]{3,2,1,0:T(8,128)}), f32[32,3,16,896]{3,2,1,0:T(8,128)}, u32[]{:S(2)}, u32[]{:S(2)}) %all-to-all-start.1) | async-done | bytes 5505056 | tf_op jit(solution)/shard_map/all_to_all | solution.py:84
  336.3 0.2 broadcast_in_dim.14
  336.5 5.2 %scatter_fusion.2 = f32[16,3,16,896]{3,2,1,0:T(8,128)S(1)} fusion(f32[16,3,16,896]{3,2,1,0:T(8,128)S(1)} %broadcast_in_dim.14, s32[32]{0:T(128)S(1)} %fusion.7, f32[32,3,16,896]{3,2,1,0:T(8,128)} %all-to-all-done.1), kind=kCustom, calls=%fused_computation.3 | custom fusion | bytes 16515200 | tf_op jit(solution)/shard_map/scatter | solution.py:50
  341.7 1.6 fusion.11
  (17 shorter events, 0.1 us)
Async XLA Ops:
  7.2 37.9 %reduce-scatter.5.cloned.1.call-start = ((), (), s32[]{:S(2)}) async-start(), calls=%async_computation.5 | async-start | bytes 1032192 | tf_op jit(solution)/shard_map/reduce_scatter | solution.py:64
  9.2 131.9 %all-gather.2.cloned.1.call-start = ((), (), s32[]{:S(2)}) async-start(), calls=%async_computation.6 | async-start | bytes 3784704 | tf_op jit(solution)/shard_map/all_gather | solution.py:70
  45.1 133.6 %reduce-scatter.3.cloned.1.call-start = ((), (), s32[]{:S(2)}) async-start(), calls=%async_computation.4 | async-start | bytes 8257536 | tf_op jit(solution)/shard_map/reduce_scatter | solution.py:61
  51.0 0.7 copy-start.2
  51.0 12.3 %copy-start.4 = (u32[256]{0:T(256)S(1)}, u32[256]{0:T(256)}, u32[]{:S(2)}) copy-start(u32[256]{0:T(256)} %constant.77) | copy-start | bytes 3076
  51.0 13.6 %copy-start.3 = (s32[2]{0:T(128)S(1)}, s32[2]{0:T(128)}, u32[]{:S(2)}) copy-start(s32[2]{0:T(128)} %param.9) | copy-start | bytes 28
  51.0 88.7 %copy-start = (f32[8,2,16,896]{3,2,1,0:T(8,128)S(1)}, f32[8,2,16,896]{3,2,1,0:T(8,128)}, u32[]{:S(2)}) copy-start(f32[8,2,16,896]{3,2,1,0:T(8,128)} %param.12) | copy-start | bytes 2752516
  53.5 146.7 %all-to-all-start = ((f32[32,1,1]{2,1,0:T(1,128)}), f32[32,1,1]{2,1,0:T(1,128)S(1)}, u32[]{:S(2)}, u32[]{:S(2)}) async-start(f32[32,1,1]{2,1,0:T(1,128)} %copy.30), calls=%async_computation | async-start | bytes 32768 | tf_op jit(solution)/shard_map/all_to_all | solution.py:85
  178.7 12.4 %copy-start.1 = (f32[8,2,16,896]{3,2,1,0:T(8,128)S(1)}, f32[8,2,16,896]{3,2,1,0:T(8,128)}, u32[]{:S(2)}) copy-start(f32[8,2,16,896]{3,2,1,0:T(8,128)} %param.10) | copy-start | bytes 2752516
  200.1 136.2 %all-to-all-start.1 = ((f32[32,3,16,896]{3,2,1,0:T(8,128)}), f32[32,3,16,896]{3,2,1,0:T(8,128)}, u32[]{:S(2)}, u32[]{:S(2)}) async-start(f32[32,3,16,896]{3,2,1,0:T(8,128)} %scatter_fusion.1), calls=%async_computation.3 | async-start | bytes 11010048 | tf_op jit(solution)/shard_map/all_to_all | solution.py:84
Sparse Core Ops, SparseCore 0:
  11.1 33.8 reduce-scatter.4
  48.0 82.7 all-gather.1
  133.5 45.0 reduce-scatter.2
where the time goes:
time: 355 us; the launch traced here: 350 us
  waiting for transfers between devices  199 us (56%)
  blocking collectives  75 us (21%)
  other arithmetic  24.3 us (7%)
  starting transfers between devices  19.8 us (6%)
  local copies, waits for them, and re-layouts  16.8 us (5%)
  between operations  14.5 us (4%)
    all_to_all x1, waiting for transfers between devices, per_device(): lax.all_to_all(outgoing, 'expert', split_axis=0, concat_axis=0, tiled=True)  126 us
    unnamed x1, blocking collectives  75 us
    reduce_scatter x1, waiting for transfers between devices, per_device(): lax.psum_scatter(partial_grads[0].astype(jnp.float32), 'dp', scatter_dime...  37.5 us
    reduce_scatter x1, waiting for transfers between devices, per_device(): lax.psum_scatter(replica_grads[0].astype(jnp.float32), 'dp', scatter_dime...  35.8 us
    scatter-add x1, other arithmetic, per_device(): flattened.at[jnp.where(inside, local_ids, item_count)]  12.3 us
    all_to_all x1, starting transfers between devices, per_device(): lax.all_to_all(labels, 'expert', split_axis=0, concat_axis=0, tiled=True)  9.86 us
    all_to_all x1, starting transfers between devices, per_device(): lax.all_to_all(outgoing, 'expert', split_axis=0, concat_axis=0, tiled=True)  9.83 us
  transfers between devices with their start and end apart: 5, of which 3 were waited for; matrix products, arithmetic and copies ran while one was open for 9% of the time, Pallas kernels for 0%

commit v1 on v0

v1 whole, which is shorter than its diff:
```python
import functools

import jax
import jax.numpy as jnp
from jax import lax
from jax.experimental import pallas as pl
from jax.experimental.pallas import tpu as pltpu
from jax.sharding import PartitionSpec as P

STEP = 10

beta_one = 0.9
beta_two = 0.95
learn_rate = 0.003
decay_rate = 0.1
epsilon = 1e-08

MESH = pl.DeviceIdType.MESH
NZ, NY, NX = 8, 4, 4
NE = NZ * NY
ITEMS = 16
CHUNKS = 9
R, C = 16, 896

ORDER = [dz * NY + dy for dz in (1, 7, 2, 6, 3, 5, 4, 0) for dy in (0, 1, 3, 2) if (dz, dy) != (0, 0)]


def kernel(
    pos_s, rit_s, rg_h, pg_h, w_h, m_h, v_h,
    ow, om, ov,
    gr, w_v, m_v, v_v, cs, cr, ra, rb, sm, ag, ch, sw, smv, rw, rmv,
    info, infos, tab, inv_s, tab_s,
    ld, tabsem, core_ss, core_rs, a_ss, a_rs, b_ss, b_rs,
    i_ss, i_rs, w_ss, w_rs, mv_ss, mv_rs, gz_ss, gz_rs, gy_ss, gy_rs, gf_ss, gf_rs,
):
    e = lax.axis_index("expert")
    d = lax.axis_index("dp")
    z, y = e // NY, e % NY
    x, c = d // 2, d % 2
    x_next, x_prev, x_far = (x + 1) % NX, (x + 3) % NX, (x + 2) % NX

    def holder(q):
        return ((z + q // NY) % NZ) * NY + (y + q % NY) % NY

    def at_expert(index):
        return (index, d)

    def at_x(index):
        return (e, index * 2 + c)

    other_core = (e, x * 2 + 1 - c)

    loads = [
        pltpu.make_async_copy(rg_h, gr.at[pl.ds(0, 2)], ld.at[0]),
        pltpu.make_async_copy(w_h, w_v, ld.at[9]),
        *[
            pltpu.make_async_copy(pg_h.at[pl.ds(2 * i - 2, 2)], gr.at[pl.ds(2 * i, 2)], ld.at[i])
            for i in range(1, CHUNKS)
        ],
        pltpu.make_async_copy(m_h, m_v, ld.at[10]),
        pltpu.make_async_copy(v_h, v_v, ld.at[11]),
    ]
    for load in loads:
        load.start()
    gr_loads = [loads[0]] + loads[2:10]

    sub = lax.broadcasted_iota(jnp.int32, (8, 128), 0)
    lane = lax.broadcasted_iota(jnp.int32, (8, 128), 1)
    tile = jnp.where(sub == 0, -1, 0)
    for j in range(ITEMS):
        place = pos_s[j // 2, j % 2]
        hit = lane == place // ITEMS
        tile = jnp.where(hit & (sub == 0), place % ITEMS, tile)
        tile = jnp.where(hit & (sub == 2), j, tile)
    for k in range(2):
        tile = jnp.where((sub == 1) & (lane == k), rit_s[k], tile)
    info[...] = tile
    infos[0] = tile
    inv_copy = pltpu.make_async_copy(info, inv_s, tabsem.at[0])
    inv_copy.start()

    barrier = pltpu.get_barrier_semaphore()
    for q in ORDER:
        pl.semaphore_signal(barrier, inc=1, device_id=at_expert(holder(q)), device_id_type=MESH)
    for peer in (other_core, at_x(x_next), at_x(x_prev)):
        pl.semaphore_signal(barrier, inc=1, device_id=peer, device_id_type=MESH)
    pl.semaphore_wait(barrier, NE - 1 + 3)

    sends = []

    def send(src, dst, ss, rs, peer):
        copy = pltpu.make_async_remote_copy(
            src_ref=src, dst_ref=dst, send_sem=ss, recv_sem=rs, device_id=peer, device_id_type=MESH
        )
        copy.start()
        sends.append(copy)
        return copy

    core_copy, a_copy, b_copy = {}, {}, {}

    def stage_core(i):
        gr_loads[i].wait()
        for xd in range(NX):
            columns = pl.ds(pl.multiple_of((xd * 2 + 1 - c) * C, 128), C)
            for u in range(2):
                cs[i, xd, u] = gr[2 * i + u, :, columns].astype(jnp.float32)
        core_copy[i] = send(cs.at[i], cr.at[i], core_ss.at[i], core_rs.at[i], other_core)

    def stage_a(i):
        core_copy[i].wait_recv()
        for xd in range(NX):
            columns = pl.ds(pl.multiple_of((xd * 2 + c) * C, 128), C)
            for u in range(2):
                cr[i, xd, u] = cr[i, xd, u] + gr[2 * i + u, :, columns].astype(jnp.float32)
        a_copy[i] = (
            send(cr.at[i, x_far, 0], ra.at[i, 0], a_ss.at[i, 0], a_rs.at[i, 0], at_x(x_next)),
            send(cr.at[i, x_far, 1], ra.at[i, 1], a_ss.at[i, 1], a_rs.at[i, 1], at_x(x_prev)),
        )

    def stage_b(i):
        a_copy[i][0].wait_recv()
        cr[i, x_next, 0] = cr[i, x_next, 0] + ra[i, 0]
        a_copy[i][1].wait_recv()
        cr[i, x_prev, 1] = cr[i, x_prev, 1] + ra[i, 1]
        b_copy[i] = (
            send(cr.at[i, x_next], rb.at[i, 0], b_ss.at[i, 0], b_rs.at[i, 0], at_x(x_next)),
            send(cr.at[i, x_prev], rb.at[i, 1], b_ss.at[i, 1], b_rs.at[i, 1], at_x(x_prev)),
        )

    def stage_sum(i):
        b_copy[i][0].wait_recv()
        b_copy[i][1].wait_recv()
        for u in range(2):
            total = cr[i, x, u] + rb[i, 0, u] + rb[i, 1, u]
            if i == 0:
                ag[0, 0, u] = total
            else:
                sm[2 * i - 2 + u] = total

    w_copy = {}

    def send_w(q):
        to = holder(q)
        sw[q] = w_v[inv_s[2, to]]
        w_copy[q] = send(sw.at[q], rw.at[q], w_ss.at[q], w_rs.at[q], at_expert(to))

    w_left = list(ORDER)

    def send_some_w(count):
        for _ in range(min(count, len(w_left))):
            send_w(w_left.pop(0))

    gz_copy, gy_copy, gf_copy = {}, {}, {}

    def gather_z():
        for dz in (4, 3, 5, 2, 6, 1, 7):
            gz_copy[dz] = send(ag.at[0, 0], ag.at[0, dz], gz_ss.at[dz], gz_rs.at[dz], at_expert(holder(dz * NY)))

    def gather_y(dz):
        if dz:
            gz_copy[dz].wait_recv()
        gy_copy[dz] = (
            send(ag.at[0, dz], ag.at[1, dz], gy_ss.at[dz, 0], gy_rs.at[dz, 0], at_expert(holder(1))),
            send(ag.at[0, dz], ag.at[3, dz], gy_ss.at[dz, 1], gy_rs.at[dz, 1], at_expert(holder(3))),
        )

    def forward_y(dz):
        gy_copy[dz][0].wait_recv()
        gy_copy[dz][1].wait_recv()
        if dz % 2:
            gf_copy[dz] = send(ag.at[1, dz], ag.at[2, dz], gf_ss.at[dz], gf_rs.at[dz], at_expert(holder(1)))
        else:
            gf_copy[dz] = send(ag.at[3, dz], ag.at[2, dz], gf_ss.at[dz], gf_rs.at[dz], at_expert(holder(3)))

    stage_core(0)
    stage_core(1)
    i_copy = {}
    for q in ORDER:
        i_copy[q] = send(info, infos.at[q], i_ss.at[q], i_rs.at[q], at_expert(holder(q)))
    stage_a(0)
    loads[1].wait()
    inv_copy.wait()
    send_some_w(4)
    stage_b(0)
    stage_core(2)
    stage_a(1)
    send_some_w(4)
    stage_b(1)
    stage_core(3)
    stage_a(2)
    stage_sum(0)
    gather_z()
    gather_y(0)
    for i in range(2, CHUNKS):
        send_some_w(4)
        stage_b(i)
        if i + 2 < CHUNKS:
            stage_core(i + 2)
        if i + 1 < CHUNKS:
            stage_a(i + 1)
        stage_sum(i - 1)
        if i == 5:
            for dz in (1, 7, 2, 6, 3, 5, 4):
                gather_y(dz)
    send_some_w(NE)
    stage_sum(CHUNKS - 1)
    for dz in (0, 1, 7, 2, 6, 3, 5, 4):
        forward_y(dz)

    for q in ORDER:
        i_copy[q].wait_recv()
    sub = lax.broadcasted_iota(jnp.int32, (NE, 128), 0)
    lane = lax.broadcasted_iota(jnp.int32, (NE, 128), 1)
    places = jnp.sum(jnp.where(lane == e, infos[:, 0, :], 0), axis=1, keepdims=True)
    tab[0:1, :] = jnp.max(jnp.where(places == lane, sub, 0), axis=0, keepdims=True)
    served = infos[:, 1, :]
    first_slot = jnp.sum(jnp.where(lane == 0, served, 0), axis=1, keepdims=True)
    second_slot = jnp.sum(jnp.where(lane == 1, served, 0), axis=1, keepdims=True)
    column = jnp.concatenate([first_slot, second_slot], axis=0)
    sub = lax.broadcasted_iota(jnp.int32, (2 * NE, 128), 0)
    lane = lax.broadcasted_iota(jnp.int32, (2 * NE, 128), 1)
    row = jnp.sum(jnp.where(sub == lane, column, 0), axis=0, keepdims=True)
    tab[1:2, :] = jnp.max(jnp.where((column == row) & (sub < lane), sub + 1, 0), axis=0, keepdims=True)
    tab[2:3, :] = jnp.max(jnp.where(column == lane + e * ITEMS, sub + 1, 0), axis=0, keepdims=True)
    tab[3:8, :] = jnp.zeros((5, 128), jnp.int32)
    tab_copy = pltpu.make_async_copy(tab, tab_s, tabsem.at[1])
    tab_copy.start()
    loads[10].wait()
    loads[11].wait()
    tab_copy.wait()
    for dz in range(NZ):
        gf_copy[dz].wait_recv()

    ch[0] = jnp.zeros((R, C), jnp.float32)
    for r in range(2 * NE):
        k, q = r // NE, r % NE
        ch[r + 1] = ag[q % NY, q // NY, k] + ch[tab_s[1, r]]

    def moments(q, to, dst):
        j = inv_s[2, to]
        gradient = sm[j] + ch[tab_s[2, j]]
        dst[q, 0] = beta_one * m_v[j] + (1.0 - beta_one) * gradient
        dst[q, 1] = beta_two * v_v[j] + (1.0 - beta_two) * gradient * gradient

    mv_copy = {}
    for q in ORDER:
        to = holder(q)
        moments(q, to, smv)
        mv_copy[q] = send(smv.at[q], rmv.at[q], mv_ss.at[q], mv_rs.at[q], at_expert(to))
    moments(0, e, rmv)
    rw[0] = w_v[inv_s[2, e]]

    for q in ORDER:
        w_copy[q].wait_recv()
    for q in ORDER:
        mv_copy[q].wait_recv()
    for p in range(ITEMS):
        q = tab_s[0, p]
        first, second, weight = rmv[q, 0], rmv[q, 1], rw[q]
        om[p] = first
        ov[p] = second
        first_hat = first / (1.0 - beta_one**STEP)
        second_hat = second / (1.0 - beta_two**STEP)
        ow[p] = weight - learn_rate * (
            first_hat / (jnp.sqrt(second_hat) + epsilon) + decay_rate * weight
        )
    for copy in sends:
        copy.wait_send()


def per_device(
    partial_grads, replica_grads, replica_item, weight, first_moment, second_moment, new_position
):
    f32, i32, bf16 = jnp.float32, jnp.int32, jnp.bfloat16
    vmem, smem, dma = pltpu.VMEM, pltpu.SMEM, pltpu.SemaphoreType.DMA
    slab = (R, C)
    anywhere = pl.BlockSpec(memory_space=pl.ANY)
    in_smem = pl.BlockSpec(memory_space=pltpu.SMEM)
    in_vmem = pl.BlockSpec(memory_space=pltpu.VMEM)
    outs = pl.pallas_call(
        kernel,
        out_shape=[jax.ShapeDtypeStruct((ITEMS, *slab), f32)] * 3,
        in_specs=[in_smem, in_smem] + [anywhere] * 5,
        out_specs=[in_vmem] * 3,
        scratch_shapes=[
            vmem((2 * CHUNKS, R, 8 * C), bf16),
            vmem((ITEMS, *slab), f32),
            vmem((ITEMS, *slab), f32),
            vmem((ITEMS, *slab), f32),
            vmem((CHUNKS, NX, 2, *slab), f32),
            vmem((CHUNKS, NX, 2, *slab), f32),
            vmem((CHUNKS, 2, *slab), f32),
            vmem((CHUNKS, 2, 2, *slab), f32),
            vmem((ITEMS, *slab), f32),
            vmem((NY, NZ, 2, *slab), f32),
            vmem((2 * NE + 1, *slab), f32),
            vmem((NE, *slab), f32),
            vmem((NE, 2, *slab), f32),
            vmem((NE, *slab), f32),
            vmem((NE, 2, *slab), f32),
            vmem((8, 128), i32),
            vmem((NE, 8, 128), i32),
            vmem((8, 128), i32),
            smem((8, 128), i32),
            smem((8, 128), i32),
            dma((12,)),
            dma((2,)),
            dma((CHUNKS,)), dma((CHUNKS,)),
            dma((CHUNKS, 2)), dma((CHUNKS, 2)),
            dma((CHUNKS, 2)), dma((CHUNKS, 2)),
            dma((NE,)), dma((NE,)),
            dma((NE,)), dma((NE,)),
            dma((NE,)), dma((NE,)),
            dma((NZ,)), dma((NZ,)),
            dma((NZ, 2)), dma((NZ, 2)),
            dma((NZ,)), dma((NZ,)),
        ],
        name="step_and_migrate",
        compiler_params=pltpu.CompilerParams(
            collective_id=0, has_side_effects=True, vmem_limit_bytes=58 << 20
        ),
    )(
        new_position,
        replica_item,
        replica_grads[0],
        partial_grads.reshape(ITEMS, R, 8 * C),
        weight.reshape(ITEMS, *slab),
        first_moment.reshape(ITEMS, *slab),
        second_moment.reshape(ITEMS, *slab),
    )
    return tuple(out.reshape(weight.shape) for out in outs)


def solution(mesh):
    in_specs = (
        P("dp", "expert", None, None, None),
        P("dp", "expert", None, None),
        P("expert"),
        P("expert", None, None, "dp"),
        P("expert", None, None, "dp"),
        P("expert", None, None, "dp"),
        P("expert", None),
    )
    out_specs = (
        P("expert", None, None, "dp"),
        P("expert", None, None, "dp"),
        P("expert", None, None, "dp"),
    )
    return jax.shard_map(
        per_device, mesh=mesh, in_specs=in_specs, out_specs=out_specs, check_vma=False
    )
```

time: 355 us -> 184 us (0.52); the launches traced: 350 us -> 184 us
  waiting for transfers between devices: 199 us -> 0 us
  Pallas kernels: 0 us -> 177 us
  blocking collectives: 75 us -> 0 us
  other arithmetic: 24.3 us -> 0 us
  starting transfers between devices: 19.8 us -> 0 us
  between operations: 14.5 us -> 0.65 us
  local copies, waits for them, and re-layouts: 16.8 us -> 6.68 us
    pallas_call x0 -> x1, Pallas kernels: none -> 177 us  [per_device(): pl.pallas_call(kernel, out_shape=[jax.ShapeDtypeStruct((ITEMS, *slab), f3...]
    all_to_all x2 -> x0, waiting for transfers between devices: 126 us -> none  [the longest x1 126 us: per_device(): lax.all_to_all(outgoing, 'expert', split_axis=0, concat_axis=0, tiled=True)]
    unnamed x1 -> x0, blocking collectives: 75 us -> none
    reduce_scatter x2 -> x0, waiting for transfers between devices: 73.3 us -> none  [the longest x1 37.5 us: per_device(): lax.psum_scatter(partial_grads[0].astype(jnp.float32), 'dp', scatter_dime...]
    all_to_all x2 -> x0, starting transfers between devices: 19.7 us -> none  [the longest x1 9.86 us: per_device(): lax.all_to_all(labels, 'expert', split_axis=0, concat_axis=0, tiled=True)]
    scatter-add x1 -> x0, other arithmetic: 12.3 us -> none  [per_device(): flattened.at[jnp.where(inside, local_ids, item_count)]]
    scatter x3 -> x0, local copies, waits for them, and re-layouts: 10 us -> none  [the longest x1 5.22 us: unpack_slots(): return empty.at[target_row].set(received, mode='drop')]
    convert_element_type x3 -> x0, other arithmetic: 7.9 us -> none  [the longest x1 5.88 us: per_device(): partial_grads[0].astype(jnp.float32)]
  transfers between devices with their start and end apart: 5 -> 0, of which waited for: 3 -> 0; matrix products, arithmetic and copies ran while one was open for 9% -> 0% of each run, Pallas kernels for 0% -> 0%
where the time goes in v1:
time: 184 us
  Pallas kernels  177 us (96%)
  local copies, waits for them, and re-layouts  6.68 us (4%)
    pallas_call x1, Pallas kernels, per_device(): pl.pallas_call(kernel, out_shape=[jax.ShapeDtypeStruct((ITEMS, *slab), f3...  177 us
    unnamed x6, local copies, waits for them, and re-layouts  6.68 us

profile of v1, /device:TPU:6, one launch (start us, length us, event | category | flops | bytes accessed | tf_op | source)
XLA Modules:
  0.0 183.8 jit_solution(10985894305391297335)
XLA Ops:
  0.6 1.3 copy.10.pos_s
  2.0 176.5 %step_and_migrate.1 = (f32[16,16,896]{2,1,0:T(8,128)}, f32[16,16,896]{2,1,0:T(8,128)}, f32[16,16,896]{2,1,0:T(8,128)}) custom-call(s32[8,2]{1,0:T(8,128)} %copy.10.pos_s, s32[2]{0:T(128)} %rit_s.1, bf16[2,16,7168]{2,1,0:T(8,128)(2,1)} %bitcast.15, bf16[16,16,7168]{2,1,0:T(8,128)(2,1)} %bitcast.8, f32[16,16,896]{2,1,0:T(8,128)} %bitcast.9, ...), custom_call_target="tpu_custom_call" | custom-call | tf_op jit(solution)/shard_map/step_and_migrate/pallas_call | solution.py:280
  178.5 0.0 copy-start
  178.5 2.2 %copy.14 = f32[8,2,16,896]{3,2,1,0:T(8,128)} copy(f32[8,2,16,896]{3,2,1,0:T(8,128)} %bitcast.14) | data formatting | bytes 1835008
  180.8 2.2 %copy.15 = f32[8,2,16,896]{3,2,1,0:T(8,128)} copy(f32[8,2,16,896]{3,2,1,0:T(8,128)} %bitcast.13) | data formatting | bytes 1835008
  182.9 0.0 copy-done
  182.9 0.9 copy.16
Async XLA Ops:
  178.5 4.4 %copy-start = (f32[16,16,896]{2,1,0:T(8,128)S(1)}, f32[16,16,896]{2,1,0:T(8,128)}, u32[]{:S(2)}) copy-start(f32[16,16,896]{2,1,0:T(8,128)} %get-tuple-element.8) | copy-start | bytes 2752516

commit v2 on v1

v2 whole, which is shorter than its diff:
```python
import functools

import jax
import jax.numpy as jnp
from jax import lax
from jax.experimental import pallas as pl
from jax.experimental.pallas import tpu as pltpu
from jax.sharding import PartitionSpec as P

STEP = 10

beta_one = 0.9
beta_two = 0.95
learn_rate = 0.003
decay_rate = 0.1
epsilon = 1e-08

MESH = pl.DeviceIdType.MESH
NZ, NY, NX = 8, 4, 4
NE = NZ * NY
ITEMS = 16
SLABS = ITEMS + 2
CHUNKS = (
    (0, 2, 0, 16), (2, 4, 0, 8), (6, 4, 0, 8), (10, 4, 0, 8), (14, 4, 0, 8), (2, 8, 8, 8), (10, 8, 8, 8),
)
R, C = 16, 896
H = R // 2

FAR = (0, 1, 7, 2, 6, 3, 5, 4)
ARRIVAL = (0, 1, 3, 2)
GROUPS = ((0, 1), (1, 2), (3, 2), (5, 3))
STRAIGHT = list(range(1, NZ))
ACROSS = [dy * NZ + a for a in (1, 2, 3, 4, 5, 6, 7, 0) for dy in (1, 3)]
OPPOSITE = [2 * NZ + a for a in (1, 2, 3, 4, 5, 6, 7, 0)]
ORDER = [dy * NZ + a for a in (1, 2, 3, 4, 5, 6, 7, 0) for dy in (0, 1, 3, 2) if (a, dy) != (0, 0)]


def kernel(
    pos_s, rit_s, rg_h, pg_h, w_h, m_h, v_h,
    rw, rmv, tab_o,
    gr, w_v, m_v, v_v, cs, cr, ra, rb, sm, ag, ch, sw, smv,
    info, infos, tab, inv_s, tab_s,
    ld, tabsem, core_ss, core_rs, a_ss, a_rs, b_ss, b_rs,
    iz_ss, iz_rs, iy_ss, iy_rs, w_ss, w_rs, mv_ss, mv_rs, gz_ss, gz_rs, gy_ss, gy_rs, gf_ss, gf_rs,
):
    e = lax.axis_index("expert")
    d = lax.axis_index("dp")
    z, y = e // NY, e % NY
    x, c = d // 2, d % 2
    x_next, x_prev, x_far = (x + 1) % NX, (x + 3) % NX, (x + 2) % NX

    def holder(q):
        return ((z + FAR[q % NZ]) % NZ) * NY + (y + q // NZ) % NY

    def at_expert(index):
        return (index, d)

    def at_x(index):
        return (e, index * 2 + c)

    other_core = (e, x * 2 + 1 - c)

    loads = [
        pltpu.make_async_copy(rg_h, gr.at[pl.ds(0, 2)], ld.at[0]),
        pltpu.make_async_copy(w_h, w_v, ld.at[9]),
        *[
            pltpu.make_async_copy(pg_h.at[pl.ds(2 * i - 2, 2)], gr.at[pl.ds(2 * i, 2)], ld.at[i])
            for i in range(1, 9)
        ],
        pltpu.make_async_copy(m_h, m_v, ld.at[10]),
        pltpu.make_async_copy(v_h, v_v, ld.at[11]),
    ]
    for load in loads:
        load.start()
    gr_loads = [loads[0]] + loads[2:10]

    sub = lax.broadcasted_iota(jnp.int32, (8, 128), 0)
    lane = lax.broadcasted_iota(jnp.int32, (8, 128), 1)
    tile = jnp.where(sub == 0, -1, 0)
    for j in range(ITEMS):
        place = pos_s[j % 2, j // 2]
        hit = lane == place // ITEMS
        tile = jnp.where(hit & (sub == 0), place % ITEMS, tile)
        tile = jnp.where(hit & (sub == 2), j, tile)
    for k in range(2):
        tile = jnp.where((sub == 1) & (lane == k), rit_s[k], tile)
    info[...] = tile
    infos[0, 0] = tile
    inv_copy = pltpu.make_async_copy(info, inv_s, tabsem.at[0])
    inv_copy.start()

    barrier = pltpu.get_barrier_semaphore()
    for q in ORDER:
        pl.semaphore_signal(barrier, inc=1, device_id=at_expert(holder(q)), device_id_type=MESH)
    for peer in (other_core, at_x(x_next), at_x(x_prev)):
        pl.semaphore_signal(barrier, inc=1, device_id=peer, device_id_type=MESH)

    sends = []

    def send(src, dst, ss, rs, peer):
        copy = pltpu.make_async_remote_copy(
            src_ref=src, dst_ref=dst, send_sem=ss, recv_sem=rs, device_id=peer, device_id_type=MESH
        )
        copy.start()
        sends.append(copy)
        return copy

    core_copy, a_copy, b_copy = {}, {}, {}

    loaded = set()

    def widen(i):
        first, count, top, rows = CHUNKS[i]
        for u in range(first, first + count):
            if u // 2 not in loaded:
                loaded.add(u // 2)
                gr_loads[u // 2].wait()
            for xd in range(NX):
                columns = pl.ds(pl.multiple_of((xd * 2 + 1 - c) * C, 128), C)
                cs[u, xd, top : top + rows] = gr[u, :, columns].astype(jnp.float32)[top : top + rows]

    def stage_core(i):
        first, count, top, rows = CHUNKS[i]
        part = (pl.ds(first, count), slice(None), pl.ds(top, rows))
        core_copy[i] = send(cs.at[part], cr.at[part], core_ss.at[i], core_rs.at[i], other_core)

    def stage_a(i):
        first, count, top, rows = CHUNKS[i]
        core_copy[i].wait_recv()
        for u in range(first, first + count):
            for xd in range(NX):
                columns = pl.ds(pl.multiple_of((xd * 2 + c) * C, 128), C)
                own = gr[u, :, columns].astype(jnp.float32)[top : top + rows]
                cr[u, xd, top : top + rows] = cr[u, xd, top : top + rows] + own
        half = count // 2
        a_copy[i] = []
        for side, to in ((0, x_next), (1, x_prev)):
            units, part = pl.ds(first + side * half, half), pl.ds(top, rows)
            a_copy[i].append(
                send(cr.at[units, x_far, part], ra.at[units, part], a_ss.at[i, side], a_rs.at[i, side], at_x(to))
            )

    def stage_b(i):
        first, count, top, rows = CHUNKS[i]
        half = count // 2
        b_copy[i] = []
        for side, to in ((0, x_next), (1, x_prev)):
            a_copy[i][side].wait_recv()
            for u in range(first + side * half, first + side * half + half):
                cr[u, to, top : top + rows] = cr[u, to, top : top + rows] + ra[u, top : top + rows]
            units, part = pl.ds(first, count), pl.ds(top, rows)
            b_copy[i].append(
                send(cr.at[units, to, part], rb.at[side, units, part], b_ss.at[i, side], b_rs.at[i, side], at_x(to))
            )

    def stage_sum(i):
        first, count, top, rows = CHUNKS[i]
        b_copy[i][0].wait_recv()
        b_copy[i][1].wait_recv()
        for u in range(first, first + count):
            part = slice(top, top + rows)
            total = cr[u, x, part] + rb[0, u, part] + rb[1, u, part]
            if i == 0:
                for h in range(2):
                    ag[h, 0, 0, u] = total[h * H : h * H + H]
            else:
                sm[u - 2, part] = total

    w_copy = {}

    def send_w(slots):
        for q in slots:
            to = holder(q)
            sw[q] = w_v[inv_s[2, to]]
            w_copy[q] = send(sw.at[q], rw.at[q], w_ss.at[q], w_rs.at[q], at_expert(to))

    iz_copy, iy_copy = {}, {}

    def info_z():
        for a in range(1, NZ):
            iz_copy[a] = send(info, infos.at[0, a], iz_ss.at[a], iz_rs.at[a], at_expert(holder(a)))

    def info_y():
        for a in range(1, NZ):
            iz_copy[a].wait_recv()
        for dy in range(1, NY):
            iy_copy[dy] = send(
                infos.at[0], infos.at[dy], iy_ss.at[dy], iy_rs.at[dy], at_expert(holder(dy * NZ))
            )

    gz_copy, gy_copy, gf_copy = {}, {}, {}

    def gather_z(h):
        for a in range(1, NZ):
            gz_copy[h, a] = send(
                ag.at[h, 0, 0], ag.at[h, 0, a], gz_ss.at[h, a], gz_rs.at[h, a], at_expert(holder(a))
            )

    def gather_y(h, g):
        first, count = GROUPS[g]
        part = pl.ds(first, count)
        for a in range(max(first, 1), first + count):
            gz_copy[h, a].wait_recv()
        gy_copy[h, g] = [
            send(
                ag.at[h, 0, part], ag.at[h, dy, part], gy_ss.at[h, g, dy], gy_rs.at[h, g, dy],
                at_expert(holder(dy * NZ)),
            )
            for dy in (1, 3)
        ]

    def forward_y(h, g):
        first, count = GROUPS[g]
        part = pl.ds(first, count)
        gy_copy[h, g][0].wait_recv()
        gy_copy[h, g][1].wait_recv()
        dy = 1 if g in (0, 3) else 3
        gf_copy[h, g] = send(
            ag.at[h, dy, part], ag.at[h, 2, part], gf_ss.at[h, g], gf_rs.at[h, g], at_expert(holder(dy * NZ))
        )

    tab_copy = pltpu.make_async_copy(tab, tab_s, tabsem.at[1])

    def tables():
        for dy in range(1, NY):
            iy_copy[dy].wait_recv()
        sub = lax.broadcasted_iota(jnp.int32, (NE, 128), 0)
        lane = lax.broadcasted_iota(jnp.int32, (NE, 128), 1)
        place_rows = jnp.concatenate([infos[dy, :, 0, :] for dy in range(NY)], axis=0)
        places = jnp.sum(jnp.where(lane == e, place_rows, 0), axis=1, keepdims=True)
        tab[0:1, :] = jnp.max(jnp.where(places == lane, sub, 0), axis=0, keepdims=True)
        served = []
        for dy in ARRIVAL:
            rows = infos[dy, :, 1, :]
            for k in range(2):
                served.append(jnp.sum(jnp.where(lane[:NZ] == k, rows, 0), axis=1, keepdims=True))
        column = jnp.concatenate(served, axis=0)
        sub = lax.broadcasted_iota(jnp.int32, (2 * NE, 128), 0)
        lane = lax.broadcasted_iota(jnp.int32, (2 * NE, 128), 1)
        row = jnp.sum(jnp.where(sub == lane, column, 0), axis=0, keepdims=True)
        tab[1:2, :] = jnp.max(jnp.where((column == row) & (sub < lane), sub + 1, 0), axis=0, keepdims=True)
        tab[2:3, :] = jnp.max(jnp.where(column == lane + e * ITEMS, sub + 1, 0), axis=0, keepdims=True)
        tab[3:8, :] = jnp.zeros((5, 128), jnp.int32)
        tab_copy.start()

    def chain(h, order):
        dy = ARRIVAL[order]
        for k in range(2):
            for a in range(NZ):
                r = (order * 2 + k) * NZ + a
                ch[h, r + 1] = ag[h, dy, a, k] + ch[h, tab_s[1, r]]

    mv_copy = {}

    def moments(h, q, to):
        j = inv_s[2, to]
        part = slice(h * H, h * H + H)
        gradient = sm[j, part] + ch[h, tab_s[2, j]]
        smv[h, q, 0] = beta_one * m_v[j, part] + (1.0 - beta_one) * gradient
        smv[h, q, 1] = beta_two * v_v[j, part] + (1.0 - beta_two) * gradient * gradient

    def send_moments(h):
        for q in ORDER:
            to = holder(q)
            moments(h, q, to)
            mv_copy[h, q] = send(
                smv.at[h, q], rmv.at[h, q], mv_ss.at[h, q], mv_rs.at[h, q], at_expert(to)
            )
        moments(h, 0, e)

    widen(0)
    widen(1)
    loads[1].wait()
    inv_copy.wait()
    pl.semaphore_wait(barrier, NE - 1 + 3)
    stage_core(0)
    stage_core(1)
    send_w(STRAIGHT)
    info_z()
    stage_a(0)
    widen(2)
    stage_core(2)
    stage_b(0)
    stage_a(1)
    widen(3)
    stage_core(3)
    stage_sum(0)
    gather_z(0)
    gather_y(0, 0)
    gather_z(1)
    stage_b(1)
    stage_a(2)
    widen(4)
    stage_core(4)
    send_w(ACROSS[:4])
    gather_y(0, 1)
    info_y()
    stage_b(2)
    stage_a(3)
    widen(5)
    stage_core(5)
    stage_sum(1)
    gather_y(0, 2)
    forward_y(0, 0)
    stage_b(3)
    stage_a(4)
    send_w(ACROSS[4:8])
    gather_y(0, 3)
    forward_y(0, 1)
    stage_sum(2)
    widen(6)
    stage_core(6)
    tables()
    send_w(ACROSS[8:])
    stage_b(4)
    stage_a(5)
    forward_y(0, 2)
    stage_sum(3)
    for h in range(2):
        ch[h, 0] = jnp.zeros((H, C), jnp.float32)
    loads[10].wait()
    loads[11].wait()
    forward_y(0, 3)
    gather_y(1, 0)
    gather_y(1, 1)
    stage_b(5)
    stage_a(6)
    gather_y(1, 2)
    gather_y(1, 3)
    stage_sum(4)
    tab_copy.wait()
    for order in range(3):
        chain(0, order)
    for g in range(len(GROUPS)):
        gf_copy[0, g].wait_recv()
    chain(0, 3)
    send_moments(0)
    for g in range(len(GROUPS)):
        forward_y(1, g)
    stage_b(6)
    send_w(OPPOSITE)
    stage_sum(5)
    stage_sum(6)
    for order in range(3):
        chain(1, order)
    for g in range(len(GROUPS)):
        gf_copy[1, g].wait_recv()
    chain(1, 3)
    send_moments(1)

    sw[0] = w_v[inv_s[2, e]]
    own = [
        pltpu.make_async_copy(smv.at[0, 0], rmv.at[0, 0], ld.at[0]),
        pltpu.make_async_copy(smv.at[1, 0], rmv.at[1, 0], ld.at[2]),
        pltpu.make_async_copy(sw.at[0], rw.at[0], ld.at[1]),
    ]
    for copy in own:
        copy.start()
    tab_o[...] = tab[...]

    for q in ORDER:
        w_copy[q].wait_recv()
    for h in range(2):
        for q in ORDER:
            mv_copy[h, q].wait_recv()
    for copy in own:
        copy.wait()
    for copy in sends:
        copy.wait_send()


def place(tab_s, rw, rmv, ow, om, ov, w_v, mv_v, o_v, w_in, mv_in, w_out, m_out, v_out):
    ins, outs = [], []
    for p in range(ITEMS):
        q = tab_s[0, p]
        ins.append([
            pltpu.make_async_copy(rmv.at[0, q], mv_v.at[:, p, pl.ds(0, H)], mv_in.at[p, 0]),
            pltpu.make_async_copy(rmv.at[1, q], mv_v.at[:, p, pl.ds(H, H)], mv_in.at[p, 1]),
            pltpu.make_async_copy(rw.at[q], w_v.at[p], w_in.at[p]),
        ])
        for copy in ins[p]:
            copy.start()
    for p in range(ITEMS):
        for copy in ins[p]:
            copy.wait()
        first, second, weight = mv_v[0, p], mv_v[1, p], w_v[p]
        first_hat = first / (1.0 - beta_one**STEP)
        second_hat = second / (1.0 - beta_two**STEP)
        o_v[p] = weight - learn_rate * (
            first_hat / (jnp.sqrt(second_hat) + epsilon) + decay_rate * weight
        )
        for src, dst, sem in (
            (mv_v.at[0, p], om.at[p], m_out.at[p]),
            (mv_v.at[1, p], ov.at[p], v_out.at[p]),
            (o_v.at[p], ow.at[p], w_out.at[p]),
        ):
            outs.append(pltpu.make_async_copy(src, dst, sem))
            outs[-1].start()
    for copy in outs:
        copy.wait()


def per_device(
    partial_grads, replica_grads, replica_item, weight, first_moment, second_moment, new_position
):
    f32, i32, bf16 = jnp.float32, jnp.int32, jnp.bfloat16
    vmem, smem, dma = pltpu.VMEM, pltpu.SMEM, pltpu.SemaphoreType.DMA
    slab, half = (R, C), (H, C)
    anywhere = pl.BlockSpec(memory_space=pl.ANY)
    in_smem = pl.BlockSpec(memory_space=pltpu.SMEM)
    in_vmem = pl.BlockSpec(memory_space=pltpu.VMEM)
    rw, rmv, tab = pl.pallas_call(
        kernel,
        out_shape=[
            jax.ShapeDtypeStruct((NE, *slab), f32),
            jax.ShapeDtypeStruct((2, NE, 2, *half), f32),
            jax.ShapeDtypeStruct((8, 128), i32),
        ],
        in_specs=[in_smem, in_smem] + [anywhere] * 5,
        out_specs=[anywhere, anywhere, in_vmem],
        scratch_shapes=[
            vmem((SLABS, R, 8 * C), bf16),
            vmem((ITEMS, *slab), f32),
            vmem((ITEMS, *slab), f32),
            vmem((ITEMS, *slab), f32),
            vmem((SLABS, NX, *slab), f32),
            vmem((SLABS, NX, *slab), f32),
            vmem((SLABS, *slab), f32),
            vmem((2, SLABS, *slab), f32),
            vmem((ITEMS, *slab), f32),
            vmem((2, NY, NZ, 2, *half), f32),
            vmem((2, 2 * NE + 1, *half), f32),
            vmem((NE, *slab), f32),
            vmem((2, NE, 2, *half), f32),
            vmem((8, 128), i32),
            vmem((NY, NZ, 8, 128), i32),
            vmem((8, 128), i32),
            smem((8, 128), i32),
            smem((8, 128), i32),
            dma((12,)),
            dma((2,)),
            dma((len(CHUNKS),)), dma((len(CHUNKS),)),
            dma((len(CHUNKS), 2)), dma((len(CHUNKS), 2)),
            dma((len(CHUNKS), 2)), dma((len(CHUNKS), 2)),
            dma((NZ,)), dma((NZ,)),
            dma((NY,)), dma((NY,)),
            dma((NE,)), dma((NE,)),
            dma((2, NE)), dma((2, NE)),
            dma((2, NZ)), dma((2, NZ)),
            dma((2, len(GROUPS), NY)), dma((2, len(GROUPS), NY)),
            dma((2, len(GROUPS))), dma((2, len(GROUPS))),
        ],
        name="step_and_migrate",
        compiler_params=pltpu.CompilerParams(
            collective_id=0, has_side_effects=True, vmem_limit_bytes=58 << 20
        ),
    )(
        new_position.T,
        replica_item,
        replica_grads[0],
        partial_grads.reshape(ITEMS, R, 8 * C),
        weight.reshape(ITEMS, *slab),
        first_moment.reshape(ITEMS, *slab),
        second_moment.reshape(ITEMS, *slab),
    )
    outs = pl.pallas_call(
        place,
        out_shape=[jax.ShapeDtypeStruct((ITEMS, *slab), f32)] * 3,
        in_specs=[in_smem, anywhere, anywhere],
        out_specs=[anywhere] * 3,
        scratch_shapes=[
            vmem((ITEMS, *slab), f32),
            vmem((2, ITEMS, *slab), f32),
            vmem((ITEMS, *slab), f32),
            dma((ITEMS,)),
            dma((ITEMS, 2)),
        ]
        + [dma((ITEMS,))] * 3,
        name="place",
        compiler_params=pltpu.CompilerParams(vmem_limit_bytes=58 << 20),
    )(tab, rw, rmv)
    return tuple(out.reshape(weight.shape) for out in outs)


def solution(mesh):
    in_specs = (
        P("dp", "expert", None, None, None),
        P("dp", "expert", None, None),
        P("expert"),
        P("expert", None, None, "dp"),
        P("expert", None, None, "dp"),
        P("expert", None, None, "dp"),
        P("expert", None),
    )
    out_specs = (
        P("expert", None, None, "dp"),
        P("expert", None, None, "dp"),
        P("expert", None, None, "dp"),
    )
    return jax.shard_map(
        per_device, mesh=mesh, in_specs=in_specs, out_specs=out_specs, check_vma=False
    )
```

time: 184 us -> 164 us (0.89)
  Pallas kernels: 177 us -> 162 us
  local copies, waits for them, and re-layouts: 6.68 us -> 0 us
    pallas_call x1 -> x2, Pallas kernels: 177 us -> 162 us  [the longest x1 158 us: per_device(): pl.pallas_call(kernel, out_shape=[jax.ShapeDtypeStruct((NE, *slab), f32),...]
    unnamed x6 -> x0, local copies, waits for them, and re-layouts: 6.68 us -> none
where the time goes in v2:
time: 164 us; the launch traced here: 163 us
  Pallas kernels  162 us (99%)
    pallas_call x1, Pallas kernels, per_device(): pl.pallas_call(kernel, out_shape=[jax.ShapeDtypeStruct((NE, *slab), f32),...  158 us
    pallas_call x1, Pallas kernels, per_device(): pl.pallas_call(place, out_shape=[jax.ShapeDtypeStruct((ITEMS, *slab), f32...  4.28 us

profile of v2, /device:TPU:6, one launch (start us, length us, event | category | flops | bytes accessed | tf_op | source)
XLA Modules:
  0.0 162.9 jit_solution(14825811457195292930)
XLA Ops:
  0.6 158.0 %step_and_migrate.1 = (f32[32,16,896]{2,1,0:T(8,128)}, f32[2,32,2,8,896]{4,3,2,1,0:T(8,128)}, s32[8,128]{1,0:T(8,128)}) custom-call(s32[2,8]{1,0:T(2,128)} %bitcast.14, s32[2]{0:T(128)} %rit_s.1, bf16[2,16,7168]{2,1,0:T(8,128)(2,1)} %bitcast.13, bf16[16,16,7168]{2,1,0:T(8,128)(2,1)} %bitcast.9, f32[16,16,896]{2,1,0:T(8,128)} %bitcast.10, ...), custom_call_target="tpu_custom_call" | custom-call | tf_op jit(solution)/shard_map/step_and_migrate/pallas_call | solution.py:412
  158.6 4.3 %place.1 = (f32[16,16,896]{2,1,0:T(8,128)}, f32[16,16,896]{2,1,0:T(8,128)}, f32[16,16,896]{2,1,0:T(8,128)}) custom-call(s32[8,128]{1,0:T(8,128)} %get-tuple-element.9.tab_s, f32[32,16,896]{2,1,0:T(8,128)} %get-tuple-element.10.rw, f32[2,32,2,8,896]{4,3,2,1,0:T(8,128)} %get-tuple-element.11.rmv), custom_call_target="tpu_custom_call" | custom-call | tf_op jit(solution)/shard_map/place/pallas_call | solution.py:466

commit v3 on v2

--- a/solution.py
+++ b/solution.py
@@ -29,10 +29,7 @@
 FAR = (0, 1, 7, 2, 6, 3, 5, 4)
 ARRIVAL = (0, 1, 3, 2)
 GROUPS = ((0, 1), (1, 2), (3, 2), (5, 3))
-STRAIGHT = list(range(1, NZ))
-ACROSS = [dy * NZ + a for a in (1, 2, 3, 4, 5, 6, 7, 0) for dy in (1, 3)]
-OPPOSITE = [2 * NZ + a for a in (1, 2, 3, 4, 5, 6, 7, 0)]
-ORDER = [dy * NZ + a for a in (1, 2, 3, 4, 5, 6, 7, 0) for dy in (0, 1, 3, 2) if (a, dy) != (0, 0)]
+ORDER = [dy * NZ + a for a in (7, 6, 5, 4, 3, 2, 1, 0) for dy in (2, 1, 3, 0) if (a, dy) != (0, 0)]
 
 
 def kernel(
@@ -41,7 +38,7 @@
     gr, w_v, m_v, v_v, cs, cr, ra, rb, sm, ag, ch, sw, smv,
     info, infos, tab, inv_s, tab_s,
     ld, tabsem, core_ss, core_rs, a_ss, a_rs, b_ss, b_rs,
-    iz_ss, iz_rs, iy_ss, iy_rs, w_ss, w_rs, mv_ss, mv_rs, gz_ss, gz_rs, gy_ss, gy_rs, gf_ss, gf_rs,
+    iz_ss, iz_rs, iy_ss, iy_rs, w_ss, w_rs, mv_ss, mv_rs, gz_ss, gz_rs, gy_ss, gy_rs,
 ):
     e = lax.axis_index("expert")
     d = lax.axis_index("dp")
@@ -51,6 +48,11 @@
 
     def holder(q):
         return ((z + FAR[q % NZ]) % NZ) * NY + (y + q // NZ) % NY
+
+    def slot_at(a, dy):
+        odd = a % 2
+        dz = odd * ((a + 1) // 2) + (1 - odd) * (NZ - a // 2)
+        return dy * NZ + a, ((z + dz) % NZ) * NY + (y + dy) % NY
 
     def at_expert(index):
         return (index, d)
@@ -90,8 +92,12 @@
     inv_copy.start()
 
     barrier = pltpu.get_barrier_semaphore()
-    for q in ORDER:
-        pl.semaphore_signal(barrier, inc=1, device_id=at_expert(holder(q)), device_id_type=MESH)
+
+    @pl.loop(0, NE - 1)
+    def _(i):
+        _, to = slot_at(NZ - 1 - i // NY, NY - 1 - i % NY)
+        pl.semaphore_signal(barrier, inc=1, device_id=at_expert(to), device_id_type=MESH)
+
     for peer in (other_core, at_x(x_next), at_x(x_prev)):
         pl.semaphore_signal(barrier, inc=1, device_id=peer, device_id_type=MESH)
 
@@ -111,11 +117,15 @@
 
     def widen(i):
         first, count, top, rows = CHUNKS[i]
-        for u in range(first, first + count):
-            if u // 2 not in loaded:
-                loaded.add(u // 2)
-                gr_loads[u // 2].wait()
-            for xd in range(NX):
+        for pair in range(first // 2, (first + count) // 2):
+            if pair not in loaded:
+                loaded.add(pair)
+                gr_loads[pair].wait()
+
+        @pl.loop(first, first + count)
+        def _(u):
+            @pl.loop(0, NX)
+            def _(xd):
                 columns = pl.ds(pl.multiple_of((xd * 2 + 1 - c) * C, 128), C)
                 cs[u, xd, top : top + rows] = gr[u, :, columns].astype(jnp.float32)[top : top + rows]
 
@@ -127,11 +137,15 @@
     def stage_a(i):
         first, count, top, rows = CHUNKS[i]
         core_copy[i].wait_recv()
-        for u in range(first, first + count):
-            for xd in range(NX):
+
+        @pl.loop(first, first + count)
+        def _(u):
+            @pl.loop(0, NX)
+            def _(xd):
                 columns = pl.ds(pl.multiple_of((xd * 2 + c) * C, 128), C)
                 own = gr[u, :, columns].astype(jnp.float32)[top : top + rows]
                 cr[u, xd, top : top + rows] = cr[u, xd, top : top + rows] + own
+
         half = count // 2
         a_copy[i] = []
         for side, to in ((0, x_next), (1, x_prev)):
@@ -146,8 +160,11 @@
         b_copy[i] = []
         for side, to in ((0, x_next), (1, x_prev)):
             a_copy[i][side].wait_recv()
-            for u in range(first + side * half, first + side * half + half):
+
+            @pl.loop(first + side * half, first + side * half + half)
+            def _(u):
                 cr[u, to, top : top + rows] = cr[u, to, top : top + rows] + ra[u, top : top + rows]
+
             units, part = pl.ds(first, count), pl.ds(top, rows)
             b_copy[i].append(
                 send(cr.at[units, to, part], rb.at[side, units, part], b_ss.at[i, side], b_rs.at[i, side], at_x(to))
@@ -157,7 +174,9 @@
         first, count, top, rows = CHUNKS[i]
         b_copy[i][0].wait_recv()
         b_copy[i][1].wait_recv()
-        for u in range(first, first + count):
+
+        @pl.loop(first, first + count)
+        def _(u):
             part = slice(top, top + rows)
             total = cr[u, x, part] + rb[0, u, part] + rb[1, u, part]
             if i == 0:
@@ -166,13 +185,20 @@
             else:
                 sm[u - 2, part] = total
 
-    w_copy = {}
-
-    def send_w(slots):
-        for q in slots:
-            to = holder(q)
+
+    def w_send(q, to):
+        return pltpu.make_async_remote_copy(
+            src_ref=sw.at[q], dst_ref=rw.at[q], send_sem=w_ss.at[q], recv_sem=w_rs.at[q],
+            device_id=at_expert(to), device_id_type=MESH,
+        )
+
+    def send_w(dys, start, stop):
+        @pl.loop(start, stop)
+        def _(i):
+            a, dy = (1 + i // len(dys)) % NZ, dys[0] + 2 * (i % len(dys))
+            q, to = slot_at(a, dy)
             sw[q] = w_v[inv_s[2, to]]
-            w_copy[q] = send(sw.at[q], rw.at[q], w_ss.at[q], w_rs.at[q], at_expert(to))
+            w_send(q, to).start()
 
     iz_copy, iy_copy = {}, {}
 
@@ -188,7 +214,7 @@
                 infos.at[0], infos.at[dy], iy_ss.at[dy], iy_rs.at[dy], at_expert(holder(dy * NZ))
             )
 
-    gz_copy, gy_copy, gf_copy = {}, {}, {}
+    gz_copy, gy_copy = {}, {}
 
     def gather_z(h):
         for a in range(1, NZ):
@@ -206,18 +232,8 @@
                 ag.at[h, 0, part], ag.at[h, dy, part], gy_ss.at[h, g, dy], gy_rs.at[h, g, dy],
                 at_expert(holder(dy * NZ)),
             )
-            for dy in (1, 3)
+            for dy in (2, 1, 3)
         ]
-
-    def forward_y(h, g):
-        first, count = GROUPS[g]
-        part = pl.ds(first, count)
-        gy_copy[h, g][0].wait_recv()
-        gy_copy[h, g][1].wait_recv()
-        dy = 1 if g in (0, 3) else 3
-        gf_copy[h, g] = send(
-            ag.at[h, dy, part], ag.at[h, 2, part], gf_ss.at[h, g], gf_rs.at[h, g], at_expert(holder(dy * NZ))
-        )
 
     tab_copy = pltpu.make_async_copy(tab, tab_s, tabsem.at[1])
 
@@ -245,10 +261,11 @@
 
     def chain(h, order):
         dy = ARRIVAL[order]
-        for k in range(2):
-            for a in range(NZ):
-                r = (order * 2 + k) * NZ + a
-                ch[h, r + 1] = ag[h, dy, a, k] + ch[h, tab_s[1, r]]
+
+        @pl.loop(0, 2 * NZ)
+        def _(i):
+            r = order * 2 * NZ + i
+            ch[h, r + 1] = ag[h, dy, i % NZ, i // NZ] + ch[h, tab_s[1, r]]
 
     mv_copy = {}
 
@@ -259,13 +276,22 @@
         smv[h, q, 0] = beta_one * m_v[j, part] + (1.0 - beta_one) * gradient
         smv[h, q, 1] = beta_two * v_v[j, part] + (1.0 - beta_two) * gradient * gradient
 
+    def moments_copy(h, q, to):
+        return pltpu.make_async_remote_copy(
+            src_ref=smv.at[h, q], dst_ref=rmv.at[h, q], send_sem=mv_ss.at[h, q], recv_sem=mv_rs.at[h, q],
+            device_id=at_expert(to), device_id_type=MESH,
+        )
+
     def send_moments(h):
+        @pl.loop(0, NE - 1)
+        def _(i):
+            q, to = slot_at(NZ - 1 - i // NY, NY - 1 - i % NY)
+            moments(h, q, to)
+            moments_copy(h, q, to).start()
+
         for q in ORDER:
-            to = holder(q)
-            moments(h, q, to)
-            mv_copy[h, q] = send(
-                smv.at[h, q], rmv.at[h, q], mv_ss.at[h, q], mv_rs.at[h, q], at_expert(to)
-            )
+            mv_copy[h, q] = moments_copy(h, q, holder(q))
+            sends.append(mv_copy[h, q])
         moments(h, 0, e)
 
     widen(0)
@@ -275,7 +301,9 @@
     pl.semaphore_wait(barrier, NE - 1 + 3)
     stage_core(0)
     stage_core(1)
-    send_w(STRAIGHT)
+    send_w((0,), 0, NZ - 1)
+    send_w((1, 3), 0, 2 * NZ)
+    send_w((2,), 0, NZ)
     info_z()
     stage_a(0)
     widen(2)
@@ -292,7 +320,6 @@
     stage_a(2)
     widen(4)
     stage_core(4)
-    send_w(ACROSS[:4])
     gather_y(0, 1)
     info_y()
     stage_b(2)
@@ -301,26 +328,20 @@
     stage_core(5)
     stage_sum(1)
     gather_y(0, 2)
-    forward_y(0, 0)
     stage_b(3)
     stage_a(4)
-    send_w(ACROSS[4:8])
     gather_y(0, 3)
-    forward_y(0, 1)
     stage_sum(2)
     widen(6)
     stage_core(6)
     tables()
-    send_w(ACROSS[8:])
     stage_b(4)
     stage_a(5)
-    forward_y(0, 2)
     stage_sum(3)
     for h in range(2):
         ch[h, 0] = jnp.zeros((H, C), jnp.float32)
     loads[10].wait()
     loads[11].wait()
-    forward_y(0, 3)
     gather_y(1, 0)
     gather_y(1, 1)
     stage_b(5)
@@ -329,23 +350,22 @@
     gather_y(1, 3)
     stage_sum(4)
     tab_copy.wait()
-    for order in range(3):
+    chain(0, 0)
+    for g in range(len(GROUPS)):
+        for copy in gy_copy[0, g]:
+            copy.wait_recv()
+    for order in range(1, NY):
         chain(0, order)
-    for g in range(len(GROUPS)):
-        gf_copy[0, g].wait_recv()
-    chain(0, 3)
     send_moments(0)
-    for g in range(len(GROUPS)):
-        forward_y(1, g)
     stage_b(6)
-    send_w(OPPOSITE)
     stage_sum(5)
     stage_sum(6)
-    for order in range(3):
+    chain(1, 0)
+    for g in range(len(GROUPS)):
+        for copy in gy_copy[1, g]:
+            copy.wait_recv()
+    for order in range(1, NY):
         chain(1, order)
-    for g in range(len(GROUPS)):
-        gf_copy[1, g].wait_recv()
-    chain(1, 3)
     send_moments(1)
 
     sw[0] = w_v[inv_s[2, e]]
@@ -359,7 +379,9 @@
     tab_o[...] = tab[...]
 
     for q in ORDER:
-        w_copy[q].wait_recv()
+        w_copy = w_send(q, holder(q))
+        w_copy.wait_recv()
+        w_copy.wait_send()
     for h in range(2):
         for q in ORDER:
             mv_copy[h, q].wait_recv()
@@ -448,7 +470,6 @@
             dma((2, NE)), dma((2, NE)),
             dma((2, NZ)), dma((2, NZ)),
             dma((2, len(GROUPS), NY)), dma((2, len(GROUPS), NY)),
-            dma((2, len(GROUPS))), dma((2, len(GROUPS))),
         ],
         name="step_and_migrate",
         compiler_params=pltpu.CompilerParams(

time: 164 us -> 165 us (level)
  no operation moved by 1% of the time
where the time goes in v3:
time: 165 us; the launch traced here: 163 us
  Pallas kernels  163 us (99%)
    pallas_call x1, Pallas kernels, per_device(): pl.pallas_call(kernel, out_shape=[jax.ShapeDtypeStruct((NE, *slab), f32),...  158 us
    pallas_call x1, Pallas kernels, per_device(): pl.pallas_call(place, out_shape=[jax.ShapeDtypeStruct((ITEMS, *slab), f32...  4.28 us

profile of v3, /device:TPU:6, one launch (start us, length us, event | category | flops | bytes accessed | tf_op | source)
XLA Modules:
  0.0 163.3 jit_solution(8474630601468890773)
XLA Ops:
  0.6 158.4 %step_and_migrate.1 = (f32[32,16,896]{2,1,0:T(8,128)}, f32[2,32,2,8,896]{4,3,2,1,0:T(8,128)}, s32[8,128]{1,0:T(8,128)}) custom-call(s32[2,8]{1,0:T(2,128)} %bitcast.14, s32[2]{0:T(128)} %rit_s.1, bf16[2,16,7168]{2,1,0:T(8,128)(2,1)} %bitcast.13, bf16[16,16,7168]{2,1,0:T(8,128)(2,1)} %bitcast.9, f32[16,16,896]{2,1,0:T(8,128)} %bitcast.10, ...), custom_call_target="tpu_custom_call" | custom-call | tf_op jit(solution)/shard_map/step_and_migrate/pallas_call | solution.py:434
  159.0 4.3 %place.1 = (f32[16,16,896]{2,1,0:T(8,128)}, f32[16,16,896]{2,1,0:T(8,128)}, f32[16,16,896]{2,1,0:T(8,128)}) custom-call(s32[8,128]{1,0:T(8,128)} %get-tuple-element.9.tab_s, f32[32,16,896]{2,1,0:T(8,128)} %get-tuple-element.10.rw, f32[2,32,2,8,896]{4,3,2,1,0:T(8,128)} %get-tuple-element.11.rmv), custom_call_target="tpu_custom_call" | custom-call | tf_op jit(solution)/shard_map/place/pallas_call | solution.py:487

commit v4 on v2

--- a/solution.py
+++ b/solution.py
@@ -32,7 +32,7 @@
 STRAIGHT = list(range(1, NZ))
 ACROSS = [dy * NZ + a for a in (1, 2, 3, 4, 5, 6, 7, 0) for dy in (1, 3)]
 OPPOSITE = [2 * NZ + a for a in (1, 2, 3, 4, 5, 6, 7, 0)]
-ORDER = [dy * NZ + a for a in (1, 2, 3, 4, 5, 6, 7, 0) for dy in (0, 1, 3, 2) if (a, dy) != (0, 0)]
+ORDER = [dy * NZ + a for a in (7, 6, 5, 4, 3, 2, 1, 0) for dy in (2, 1, 3, 0) if (a, dy) != (0, 0)]
 
 
 def kernel(
@@ -41,7 +41,7 @@
     gr, w_v, m_v, v_v, cs, cr, ra, rb, sm, ag, ch, sw, smv,
     info, infos, tab, inv_s, tab_s,
     ld, tabsem, core_ss, core_rs, a_ss, a_rs, b_ss, b_rs,
-    iz_ss, iz_rs, iy_ss, iy_rs, w_ss, w_rs, mv_ss, mv_rs, gz_ss, gz_rs, gy_ss, gy_rs, gf_ss, gf_rs,
+    iz_ss, iz_rs, iy_ss, iy_rs, w_ss, w_rs, mv_ss, mv_rs, gz_ss, gz_rs, gy_ss, gy_rs,
 ):
     e = lax.axis_index("expert")
     d = lax.axis_index("dp")
@@ -188,7 +188,7 @@
                 infos.at[0], infos.at[dy], iy_ss.at[dy], iy_rs.at[dy], at_expert(holder(dy * NZ))
             )
 
-    gz_copy, gy_copy, gf_copy = {}, {}, {}
+    gz_copy, gy_copy = {}, {}
 
     def gather_z(h):
         for a in range(1, NZ):
@@ -206,18 +206,8 @@
                 ag.at[h, 0, part], ag.at[h, dy, part], gy_ss.at[h, g, dy], gy_rs.at[h, g, dy],
                 at_expert(holder(dy * NZ)),
             )
-            for dy in (1, 3)
+            for dy in (2, 1, 3)
         ]
-
-    def forward_y(h, g):
-        first, count = GROUPS[g]
-        part = pl.ds(first, count)
-        gy_copy[h, g][0].wait_recv()
-        gy_copy[h, g][1].wait_recv()
-        dy = 1 if g in (0, 3) else 3
-        gf_copy[h, g] = send(
-            ag.at[h, dy, part], ag.at[h, 2, part], gf_ss.at[h, g], gf_rs.at[h, g], at_expert(holder(dy * NZ))
-        )
 
     tab_copy = pltpu.make_async_copy(tab, tab_s, tabsem.at[1])
 
@@ -275,7 +265,7 @@
     pl.semaphore_wait(barrier, NE - 1 + 3)
     stage_core(0)
     stage_core(1)
-    send_w(STRAIGHT)
+    send_w(STRAIGHT + ACROSS)
     info_z()
     stage_a(0)
     widen(2)
@@ -292,7 +282,6 @@
     stage_a(2)
     widen(4)
     stage_core(4)
-    send_w(ACROSS[:4])
     gather_y(0, 1)
     info_y()
     stage_b(2)
@@ -301,26 +290,21 @@
     stage_core(5)
     stage_sum(1)
     gather_y(0, 2)
-    forward_y(0, 0)
     stage_b(3)
     stage_a(4)
-    send_w(ACROSS[4:8])
     gather_y(0, 3)
-    forward_y(0, 1)
     stage_sum(2)
     widen(6)
     stage_core(6)
     tables()
-    send_w(ACROSS[8:])
     stage_b(4)
     stage_a(5)
-    forward_y(0, 2)
+    send_w(OPPOSITE)
     stage_sum(3)
     for h in range(2):
         ch[h, 0] = jnp.zeros((H, C), jnp.float32)
     loads[10].wait()
     loads[11].wait()
-    forward_y(0, 3)
     gather_y(1, 0)
     gather_y(1, 1)
     stage_b(5)
@@ -329,23 +313,22 @@
     gather_y(1, 3)
     stage_sum(4)
     tab_copy.wait()
-    for order in range(3):
+    chain(0, 0)
+    for g in range(len(GROUPS)):
+        for copy in gy_copy[0, g]:
+            copy.wait_recv()
+    for order in range(1, NY):
         chain(0, order)
-    for g in range(len(GROUPS)):
-        gf_copy[0, g].wait_recv()
-    chain(0, 3)
     send_moments(0)
-    for g in range(len(GROUPS)):
-        forward_y(1, g)
     stage_b(6)
-    send_w(OPPOSITE)
     stage_sum(5)
     stage_sum(6)
-    for order in range(3):
+    chain(1, 0)
+    for g in range(len(GROUPS)):
+        for copy in gy_copy[1, g]:
+            copy.wait_recv()
+    for order in range(1, NY):
         chain(1, order)
-    for g in range(len(GROUPS)):
-        gf_copy[1, g].wait_recv()
-    chain(1, 3)
     send_moments(1)
 
     sw[0] = w_v[inv_s[2, e]]
@@ -448,7 +431,6 @@
             dma((2, NE)), dma((2, NE)),
             dma((2, NZ)), dma((2, NZ)),
             dma((2, len(GROUPS), NY)), dma((2, len(GROUPS), NY)),
-            dma((2, len(GROUPS))), dma((2, len(GROUPS))),
         ],
         name="step_and_migrate",
         compiler_params=pltpu.CompilerParams(

time: 164 us -> 160 us (0.976)
  Pallas kernels: 162 us -> 159 us
    pallas_call x1, Pallas kernels: 158 us -> 155 us  [per_device(): pl.pallas_call(kernel, out_shape=[jax.ShapeDtypeStruct((NE, *slab), f32),...]
where the time goes in v4:
time: 160 us
  Pallas kernels  159 us (99%)
    pallas_call x1, Pallas kernels, per_device(): pl.pallas_call(kernel, out_shape=[jax.ShapeDtypeStruct((NE, *slab), f32),...  155 us
    pallas_call x1, Pallas kernels, per_device(): pl.pallas_call(place, out_shape=[jax.ShapeDtypeStruct((ITEMS, *slab), f32...  4.28 us

profile of v4, /device:TPU:6, one launch (start us, length us, event | category | flops | bytes accessed | tf_op | source)
XLA Modules:
  0.0 159.9 jit_solution(5884181184142196989)
XLA Ops:
  0.6 154.9 %step_and_migrate.1 = (f32[32,16,896]{2,1,0:T(8,128)}, f32[2,32,2,8,896]{4,3,2,1,0:T(8,128)}, s32[8,128]{1,0:T(8,128)}) custom-call(s32[2,8]{1,0:T(2,128)} %bitcast.14, s32[2]{0:T(128)} %rit_s.1, bf16[2,16,7168]{2,1,0:T(8,128)(2,1)} %bitcast.13, bf16[16,16,7168]{2,1,0:T(8,128)(2,1)} %bitcast.9, f32[16,16,896]{2,1,0:T(8,128)} %bitcast.10, ...), custom_call_target="tpu_custom_call" | custom-call | tf_op jit(solution)/shard_map/step_and_migrate/pallas_call | solution.py:395
  155.6 4.3 %place.1 = (f32[16,16,896]{2,1,0:T(8,128)}, f32[16,16,896]{2,1,0:T(8,128)}, f32[16,16,896]{2,1,0:T(8,128)}) custom-call(s32[8,128]{1,0:T(8,128)} %get-tuple-element.9.tab_s, f32[32,16,896]{2,1,0:T(8,128)} %get-tuple-element.10.rw, f32[2,32,2,8,896]{4,3,2,1,0:T(8,128)} %get-tuple-element.11.rmv), custom_call_target="tpu_custom_call" | custom-call | tf_op jit(solution)/shard_map/place/pallas_call | solution.py:448
